TPU v7x, 32 devices: a whole 2x2x4 slice. The times are simulated.
32 devices in a mesh: groups: 2 (over y), dp: 4 (over z), tensor: 4 (over x, core).
Axes of the slice: x: 2, y: 2, z: 4, core: 2. Of those that a mesh axis runs over, the one named last changes fastest.
Arguments:
- stored_input: bfloat16 [8192, 8192], P(('groups', 'dp'), 'tensor'), parts along dimension 0, may hold values from -6 to 6
- output_gradient: bfloat16 [8192, 2048], P(('groups', 'dp'), 'tensor'), parts along dimension 0, may hold values from -3 to 3
- frozen_key_value: bfloat16 [8192, 2048], P('tensor'), may hold values from -0.0625 to 0.0625
- adapter_down_weight: bfloat16 [24, 32, 8192], P('groups', None, 'tensor'), parts along dimension 0, may hold values from -0.0625 to 0.0625
- adapter_up_weight: bfloat16 [24, 32, 2048], P('groups', None, 'tensor'), parts along dimension 0, may hold values from -0.125 to 0.125
- token_tenant: int32 [8192, 1], P(('groups', 'dp')), parts along dimension 0, may hold values from 0 to 11; in each aligned block of 1024 rows (0 to 1023, 1024 to 2047, ...) at most 258 rows name the same one
- adapter_position: int32 [24], P('groups'), parts along dimension 0, may hold values from 0 to 11, each once
Outputs:
- input_gradient: bfloat16 [8192, 8192], P(('groups', 'dp'), 'tensor'), parts along dimension 0
- down_grad: float32 [24, 32, 8192], P(('groups', 'dp'), None, 'tensor'), parts along dimension 0
- up_grad: float32 [24, 32, 2048], P(('groups', 'dp'), None, 'tensor'), parts along dimension 0
There are 2 independent parts, one for each index of `groups`. A program takes and returns all parts, laid end to end along the dimension named above; an argument that names none is the same for every part. Nothing has to cross between parts.
Inputs may be any that keep to these rules, and one draw needn't show every extreme that they name: `token_tenant`: among the tokens of one index of dp no adapter is named more than 258 times, a bound that some block reaches; every adapter is named by some token of the part. `adapter_position`: A permutation: each slot holds one adapter.
All inputs are finite; a program needn't handle non-finite values.
Results may differ from a plain program's by a relative error of at most 0.0029.
Values may be sent and summed in bfloat16 or wider, within the bound.
A program may use at most 192 MiB of HBM per device.

v0:
```python
import jax
import jax.numpy as jnp
from jax import lax
from jax.sharding import PartitionSpec as P


def body(
    stored_input,
    output_gradient,
    frozen_key_value,
    adapter_down_weight,
    adapter_up_weight,
    token_tenant,
    adapter_position,
):
    tok_rows = stored_input.shape[0]
    width_local = stored_input.shape[1]
    kv_local = output_gradient.shape[1]
    adapter_list = adapter_down_weight.shape[0]
    rank_extent = adapter_down_weight.shape[1]
    owners = lax.axis_size("dp")
    per_owner = adapter_list // owners
    capacity = 3 * ((tok_rows + adapter_list - 1) // adapter_list)
    adapter_ids = token_tenant[:, 0]
    member = lax.broadcasted_iota(jnp.int32, (adapter_list, tok_rows), 0) == adapter_ids[None, :]
    home_of = jnp.sum(jnp.where(member, adapter_position[:, None], 0), axis=0)
    member_i = member.astype(jnp.int32)
    before = jnp.cumsum(member_i, axis=1) - member_i
    order_in = jnp.sum(before * member_i, axis=0)
    position_index = home_of * capacity + order_in
    placing = (
        lax.broadcasted_iota(jnp.int32, (adapter_list * capacity, tok_rows), 0)
        == position_index[None, :]
    ).astype(jnp.bfloat16)
    slot_x = (
        jnp.dot(placing, stored_input, preferred_element_type=jnp.float32)
        .astype(jnp.bfloat16)
        .reshape(adapter_list, capacity, width_local)
    )
    slot_d = (
        jnp.dot(placing, output_gradient, preferred_element_type=jnp.float32)
        .astype(jnp.bfloat16)
        .reshape(adapter_list, capacity, kv_local)
    )
    matching = (
        lax.broadcasted_iota(jnp.int32, (adapter_list, adapter_list), 0)
        == adapter_position[None, :]
    )
    position_holder = jnp.sum(
        jnp.where(matching, lax.broadcasted_iota(jnp.int32, (adapter_list, adapter_list), 1), 0),
        axis=1,
    )
    down_position = jnp.take(adapter_down_weight, position_holder, axis=0)
    up_position = jnp.take(adapter_up_weight, position_holder, axis=0)
    part_u = jnp.einsum("akd,ard->akr", slot_x, down_position, preferred_element_type=jnp.float32)
    part_g = jnp.einsum("akc,arc->akr", slot_d, up_position, preferred_element_type=jnp.float32)
    full_u, full_g = lax.psum((part_u, part_g), "tensor")
    low_u = full_u.astype(jnp.bfloat16)
    rank_gradient = full_g.astype(jnp.bfloat16)
    adapter_positions = jnp.einsum(
        "akr,ard->akd", rank_gradient, down_position, preferred_element_type=jnp.float32
    ).reshape(adapter_list * capacity, width_local)
    adapter_contribution = jnp.take(adapter_positions, position_index, axis=0)
    contract_last = (((1,), (1,)), ((), ()))
    frozen_contribution = lax.dot_general(
        lax.all_gather(output_gradient, "tensor", axis=1, tiled=True),
        frozen_key_value,
        contract_last,
        preferred_element_type=jnp.float32,
    )
    input_gradient = (frozen_contribution + adapter_contribution).astype(jnp.bfloat16)
    many = lax.axis_size("dp") * (per_owner * rank_extent) // rank_extent
    down_term = jnp.einsum(
        "akr,akd->ard", rank_gradient, slot_x, preferred_element_type=jnp.float32
    ).reshape(many * rank_extent, width_local)
    up_term = jnp.einsum("akr,akc->arc", low_u, slot_d, preferred_element_type=jnp.float32).reshape(
        many * rank_extent, kv_local
    )
    owned_rows = lax.psum_scatter(
        jnp.concatenate([down_term, up_term], axis=1), "dp", scatter_dimension=0, tiled=True
    )
    down_grad = owned_rows[:, :width_local].reshape(per_owner, rank_extent, width_local)
    up_grad = owned_rows[:, width_local:].reshape(per_owner, rank_extent, kv_local)
    return (input_gradient, down_grad, up_grad)


def solution(mesh):
    in_specs = (
        P(("groups", "dp"), "tensor"),
        P(("groups", "dp"), "tensor"),
        P("tensor", None),
        P("groups", None, "tensor"),
        P("groups", None, "tensor"),
        P(("groups", "dp"), None),
        P("groups"),
    )
    out_specs = (
        P(("groups", "dp"), "tensor"),
        P(("groups", "dp"), None, "tensor"),
        P(("groups", "dp"), None, "tensor"),
    )
    return jax.shard_map(body, mesh=mesh, in_specs=in_specs, out_specs=out_specs, check_vma=False)
```

profile of v0, /device:TPU:0, one launch (start us, length us, event | category | flops | bytes accessed | tf_op | source)
XLA Modules:
  0.0 196.9 jit_solution(1565410801189848022)
XLA Ops:
  8.0 0.0 copy-start
  8.0 0.0 all-gather.2.cloned.1.call-start
  8.1 0.7 all-gather.2.cloned.1.call-update
  8.7 0.0 reduce-scatter.2.cloned.1.call-start
  8.8 0.7 fusion.15
  9.5 3.4 %reduce-window.6 = s32[12,8,128]{2,1,0:T(8,128)S(1)} reduce-window(s32[12,8,128]{2,1,0:T(8,128)S(1)} %fusion.15, s32[]{:T(128)} %constant.42.clone.1), window={size=1x1x128 pad=0_0x0_0x127_0}, to_apply=%region_1.2 | reduce-window | flops 1560576 | bytes 98308 | tf_op jit(solution)/shard_map/reduce-window
  12.9 0.1 slice.22
  12.9 0.1 copy.12
  13.1 0.1 copy.13
  13.2 0.8 select_reduce_fusion.1
  14.0 0.8 select_reduce_fusion
  14.8 17.7 %convolution_convert_fusion = bf16[3096,2048]{1,0:T(8,128)(2,1)} fusion(bf16[1024,2048]{1,0:T(8,128)(2,1)} %param.7, s32[1024]{0:T(1024)S(1)} %get-tuple-element.6), kind=kOutput, calls=%fused_computation.3 | convolution fusion | flops 12995076096 | bytes 16879616 | tf_op jit(solution)/shard_map/dot_general | solution.py:36
  32.5 0.0 copy-start.4
  32.5 16.0 %reshape.116 = bf16[12,258,2048]{2,1,0:T(8,128)(2,1)} reshape(bf16[3096,2048]{1,0:T(8,128)(2,1)} %convolution_convert_fusion) | data formatting | bytes 25362432 | tf_op jit(solution)/shard_map/reshape | solution.py:38
  48.6 0.0 copy-done.4
  48.6 0.1 select_reduce_fusion.2
  48.7 0.0 copy-done
  48.7 0.6 gather_fusion.1
  49.4 0.0 copy-start.2
  49.4 7.9 %fusion.4 = f32[12,258,32]{1,2,0:T(8,128)} fusion(bf16[12,258,2048]{2,1,0:T(8,128)(2,1)} %reshape.116, bf16[12,32,2048]{2,1,0:T(8,128)(2,1)S(1)} %gather_fusion.1, pred[12]{0:T(512)(128)(4,1)S(1)} %compare_and_fusion.1), kind=kOutput, calls=%fused_computation.12 | convolution fusion | flops 406585344 | bytes 14650380 | tf_op jit(solution)/shard_map/akd,ard->akr/dot_general | solution.py:55
  57.3 0.0 copy-done.2
  57.3 6.1 %fusion.3 = bf16[3096,512]{1,0:T(8,128)(2,1)} fusion(bf16[1024,512]{1,0:T(8,128)(2,1)S(1)} %copy-done.2, s32[1024]{0:T(1024)S(1)} %get-tuple-element.6), kind=kOutput, calls=%fused_computation.9 | convolution fusion | flops 3251146752 | bytes 4222976 | tf_op jit(solution)/shard_map/dot_general | solution.py:41
  63.4 0.0 copy-start.3
  63.4 4.8 %reshape.114 = bf16[12,258,512]{2,1,0:T(8,128)(2,1)} reshape(bf16[3096,512]{1,0:T(8,128)(2,1)} %fusion.3) | data formatting | bytes 6340608 | tf_op jit(solution)/shard_map/reshape | solution.py:43
  68.2 0.0 copy-done.3
  68.2 0.6 gather_fusion
  68.8 3.0 %fusion.6 = f32[12,258,32]{1,2,0:T(8,128)S(1)} fusion(bf16[12,258,512]{2,1,0:T(8,128)(2,1)} %reshape.114, bf16[12,32,512]{2,1,0:T(8,128)(2,1)S(1)} %gather_fusion, pred[12]{0:T(512)(128)(4,1)S(1)} %compare_and_fusion.1), kind=kOutput, calls=%fused_computation.14 | convolution fusion | flops 101646336 | bytes 3959820 | tf_op jit(solution)/shard_map/akc,arc->akr/dot_general | solution.py:56
  71.8 29.3 %all-reduce.2 = (bf16[12,258,32]{1,2,0:T(8,128)(2,1)S(1)}, bf16[12,258,32]{1,2,0:T(8,128)(2,1)S(1)}) all-reduce(f32[12,258,32]{1,2,0:T(8,128)S(1)} %fusion.6, f32[12,258,32]{1,2,0:T(8,128)} %fusion.4), channel_id=1, replica_groups=mesh['groups'=2,'dp'=4,'tensor'=4] {'tensor'}, use_global_device_ids=true, to_apply=%region_5.6 | all-reduce | flops 198144 | bytes 1188864 | tf_op jit(solution)/shard_map/psum | solution.py:57
  101.1 2.7 %fusion.20 = f32[12,32,512]{2,1,0:T(8,128)S(1)} fusion(bf16[12,258,32]{1,2,0:T(8,128)(2,1)S(1)} %get-tuple-element.4, bf16[12,258,512]{2,1,0:T(8,128)(2,1)} %reshape.114), kind=kOutput, calls=%fused_computation.44 | convolution fusion | flops 101449728 | bytes 4154880 | tf_op jit(solution)/shard_map/akr,akc->arc/dot_general | solution.py:76
  103.8 6.2 %fusion.21 = f32[12,32,2048]{2,1,0:T(8,128)S(1)} fusion(bf16[12,258,32]{1,2,0:T(8,128)(2,1)S(1)} %get-tuple-element.3, bf16[12,258,2048]{2,1,0:T(8,128)(2,1)} %reshape.116), kind=kOutput, calls=%fused_computation.45 | convolution fusion | flops 405798912 | bytes 16025088 | tf_op jit(solution)/shard_map/akr,akd->ard/dot_general | solution.py:73
  110.0 2.3 %pad_maximum_fusion = f32[384,2560]{1,0:T(8,128)} fusion(f32[384,512]{1,0:T(8,128)S(1)} %bitcast.29, f32[384,2048]{1,0:T(8,128)S(1)} %bitcast.28), kind=kLoop, calls=%fused_computation.10 | loop fusion | flops 983040 | bytes 7864320 | tf_op jit(solution)/shard_map/concatenate | solution.py:80
  112.3 0.0 reduce-scatter.2.cloned.1.call-update
  112.3 10.9 %fusion.5 = f32[12,258,2048]{2,1,0:T(8,128)} fusion(bf16[12,32,2048]{2,1,0:T(8,128)(2,1)S(1)} %gather_fusion.1, pred[12]{0:T(512)(128)(4,1)S(1)} %compare_and_fusion.1, bf16[12,258,32]{1,2,0:T(8,128)(2,1)S(1)} %get-tuple-element.3), kind=kOutput, calls=%fused_computation.13 | convolution fusion | flops 406585344 | bytes 27133452 | tf_op jit(solution)/shard_map/akr,ard->akd/dot_general | solution.py:60
  123.2 23.2 %reshape.115 = f32[3096,2048]{1,0:T(8,128)} reshape(f32[12,258,2048]{2,1,0:T(8,128)} %fusion.5) | data formatting | bytes 50724864 | tf_op jit(solution)/shard_map/reshape | solution.py:62
  146.4 17.3 %gather_fusion.2 = f32[1024,2048]{1,0:T(8,128)} fusion(f32[3096,2048]{1,0:T(8,128)} %reshape.115, s32[1024]{0:T(1024)S(1)} %broadcast_clamp_fusion), kind=kCustom, calls=%fused_computation.2 | custom fusion | bytes 16781312 | tf_op jit(solution)/shard_map/jit(_take)/gather | solution.py:63
  163.7 0.0 all-gather.2.cloned.1.call-done
  163.7 0.0 copy-start.1
  163.7 15.2 %add_convert_fusion = bf16[1024,2048]{1,0:T(8,128)(2,1)} fusion(f32[1024,2048]{1,0:T(8,128)} %gather_fusion.2, pred[1024]{0:T(1024)(128)(4,1)S(1)} %get-tuple-element.5, bf16[1024,2048]{1,0:T(8,128)(2,1)} %all-gather.2.cloned.1.call-done, bf16[2048,2048]{1,0:T(8,128)(2,1)} %param.9), kind=kOutput, calls=%fused_computation.6 | convolution fusion | flops 8596226048 | bytes 25166848 | tf_op jit(solution)/shard_map/dot_general | solution.py:65
  178.8 6.9 %reduce-scatter.2.cloned.1.call-done = f32[96,2560]{1,0:T(8,128)} async-done(((f32[384,2560]{1,0:T(8,128)}), f32[96,2560]{1,0:T(8,128)}) %reduce-scatter.2.cloned.1.call-update) | async-done | bytes 983056 | tf_op jit(solution)/shard_map/reduce_scatter | solution.py:79
  185.7 2.1 %slice.24 = f32[96,2048]{1,0:T(8,128)} slice(f32[96,2560]{1,0:T(8,128)} %reduce-scatter.2.cloned.1.call-done), slice={[0:96], [0:2048]} | slice | bytes 1572864 | tf_op jit(solution)/shard_map/slice | solution.py:82
  187.8 1.6 slice.25
  189.4 0.0 copy-done.1
  (9 shorter events, 0.1 us)
Async XLA Ops:
  8.0 40.7 %copy-start = (bf16[12,32,2048]{2,1,0:T(8,128)(2,1)S(1)}, bf16[12,32,2048]{2,1,0:T(8,128)(2,1)}, u32[]{:S(2)}) copy-start(bf16[12,32,2048]{2,1,0:T(8,128)(2,1)} %param.10) | copy-start | bytes 4718596
  8.0 155.6 %all-gather.2.cloned.1.call-start = ((), (), s32[]{:S(2)}) async-start(), calls=%async_computation.1 | async-start | bytes 5242880 | tf_op jit(solution)/shard_map/all_gather | solution.py:66
  8.7 177.0 %reduce-scatter.2.cloned.1.call-start = ((), (), s32[]{:S(2)}) async-start(), calls=%async_computation.2 | async-start | bytes 4915200 | tf_op jit(solution)/shard_map/reduce_scatter | solution.py:79
  32.5 16.0 %copy-start.4 = (s32[12]{0:T(128)S(1)}, s32[12]{0:T(128)}, u32[]{:S(2)}) copy-start(s32[12]{0:T(128)} %param.13) | copy-start | bytes 148
  49.4 7.9 %copy-start.2 = (bf16[1024,512]{1,0:T(8,128)(2,1)S(1)}, bf16[1024,512]{1,0:T(8,128)(2,1)}, u32[]{:S(2)}) copy-start(bf16[1024,512]{1,0:T(8,128)(2,1)} %param.8) | copy-start | bytes 3145732
  63.4 4.8 %copy-start.3 = (bf16[12,32,512]{2,1,0:T(8,128)(2,1)S(1)}, bf16[12,32,512]{2,1,0:T(8,128)(2,1)}, u32[]{:S(2)}) copy-start(bf16[12,32,512]{2,1,0:T(8,128)(2,1)} %param.11) | copy-start | bytes 1179652
  163.7 25.8 %copy-start.1 = (bf16[12,32,2048]{2,1,0:T(8,128)(2,1)S(1)}, bf16[12,32,2048]{2,1,0:T(8,128)(2,1)}, u32[]{:S(2)}) copy-start(bf16[12,32,2048]{2,1,0:T(8,128)(2,1)} %param.10) | copy-start | bytes 4718596
Sparse Core Ops, SparseCore 0:
  10.4 37.1 all-gather.1
Sparse Core Ops, SparseCore 1:
  112.4 73.3 reduce-scatter.1
where the time goes:
time: 198 us; the launch traced here: 197 us
  matrix products  69.6 us (35%)
  local copies, waits for them, and re-layouts  66.5 us (34%)
  blocking collectives  29.3 us (15%)
  between operations  15.6 us (8%)
  other arithmetic  8.12 us (4%)
  waiting for transfers between devices  7.6 us (4%)
    psum x1, blocking collectives, body(): full_u, full_g = lax.psum((part_u, part_g), 'tensor')  29.3 us
    reshape x1, local copies, waits for them, and re-layouts, body(): adapter_positions = jnp.einsum('akr,ard->akd', rank_gradient, down_positi...  23.2 us
    dot_general x1, matrix products, body(): jnp.dot(placing, stored_input, preferred_element_type=jnp.float32)  17.7 us
    gather x1, local copies, waits for them, and re-layouts, body(): adapter_contribution = jnp.take(adapter_positions, position_index, axis=0)  17.3 us
    reshape x1, local copies, waits for them, and re-layouts, body(): slot_x = jnp.dot(placing, stored_input, preferred_element_type=jnp.float3...  16 us
    dot_general x1, matrix products, body(): lax.dot_general(lax.all_gather(output_gradient, 'tensor', axis=1, tiled=T...  15.2 us
    dot_general x1, matrix products, body(): jnp.einsum('akr,ard->akd', rank_gradient, down_position, preferred_elemen...  10.9 us
    dot_general x1, matrix products, body(): jnp.einsum('akd,ard->akr', slot_x, down_position, preferred_element_type=...  7.9 us
  transfers between devices with their start and end apart: 2, of which 1 were waited for; matrix products, arithmetic and copies ran while one was open for 71% of the time, Pallas kernels for 0%

commit v1 on v0

v1 whole, which is shorter than its diff:
```python
import functools

import jax
import jax.numpy as jnp
from jax import lax
from jax.experimental import pallas as pl
from jax.experimental.pallas import tpu as pltpu
from jax.sharding import PartitionSpec as P

MESH = pl.DeviceIdType.MESH
F32 = jnp.float32
BF16 = jnp.bfloat16
LANES = 128
LAST = (((1,), (1,)), ((), ()))
HALVES = 2
WINDOW = 3


def kernel(nt, nz, rank, x_h, dy_h, w_h, d_h, u_h, tt, pos, ig_h, dg_h, ug_h,
           x, dy, w, d, u, ab, a_t, packed, landed, low, ge, ge_t, ue_t, own, acc, ig,
           r_out, r_in, l_out, l_in, dg, ug,
           load_sem, part_s, part_r, low_s, low_r, dy_s, dy_r, rs_s, rs_r, ls_s, ls_r, out_sem):
    me = lax.axis_index("tensor")
    z = lax.axis_index("dp")
    rows, width = x.shape
    kv = dy.shape[2]
    ar = d.shape[0]
    per = ar // nz
    tiles = ar // LANES
    fold = LANES // rank
    chunk_rows = rows // fold
    down_chunks = width // kv
    chunks = down_chunks + 1
    half = rows // HALVES
    chips = nt // 2
    core = lax.rem(me, 2)
    chip = me // 2
    partner = chip * 2 + 1 - core

    loads = [
        pltpu.make_async_copy(src, dst, load_sem.at[i])
        for i, (src, dst) in enumerate(
            [(u_h, u), (dy_h, dy.at[me]), (d_h, d), (x_h, x), (w_h, w)]
        )
    ]
    for load in loads:
        load.start()

    barrier = pltpu.get_barrier_semaphore()
    for off in range(1, nt):
        pl.semaphore_signal(barrier, inc=1, device_id={"tensor": lax.rem(me + off, nt)},
                            device_id_type=MESH)

    @pl.when(z > 0)
    def _():
        pl.semaphore_signal(barrier, inc=1, device_id={"dp": z - 1}, device_id_type=MESH)

    @pl.when(z < nz - 1)
    def _():
        pl.semaphore_signal(barrier, inc=1, device_id={"dp": z + 1}, device_id_type=MESH)

    for i in range(rows // LANES):
        row = jnp.broadcast_to(tt[i : i + 1, :].astype(F32), (LANES, LANES))
        a_t[:, i * LANES : (i + 1) * LANES] = row[0:8, :]
        ab[i * LANES : (i + 1) * LANES, :] = row.T

    group_of = (lax.broadcasted_iota(jnp.int32, (chunk_rows, LANES), 1) // rank).astype(F32)
    group_t = (lax.broadcasted_iota(jnp.int32, (LANES, chunk_rows), 0) // rank).astype(F32)

    def spread(v):
        step = LANES // 2
        while step >= rank:
            v = v + pltpu.roll(v, step, 1)
            step //= 2
        return v

    def project(kind, source, weight):
        total = jnp.zeros((chunk_rows, LANES), F32)
        for k in range(fold):
            part = lax.dot_general(source(k), weight[...], LAST, preferred_element_type=F32)
            a_k = ab[k * chunk_rows : (k + 1) * chunk_rows, :]
            mine = jnp.zeros((chunk_rows, LANES), F32)
            for j in range(tiles):
                mine = mine + jnp.where(
                    a_k == group_of + float(fold * j), part[:, j * LANES : (j + 1) * LANES], 0.0
                )
            total = jnp.where(group_of == float(k), spread(mine), total)
        packed[kind] = total.reshape(packed.shape[1:])

    def part_copy(kind, off, src_slot, dst_slot):
        return pltpu.make_async_remote_copy(
            src_ref=packed.at[kind, src_slot], dst_ref=landed.at[kind, dst_slot],
            send_sem=part_s.at[kind, off], recv_sem=part_r.at[kind, off],
            device_id={"tensor": lax.rem(me + off, nt)}, device_id_type=MESH)

    def low_copy(kind, off, slot):
        return pltpu.make_async_remote_copy(
            src_ref=low.at[kind, slot], dst_ref=low.at[kind, slot],
            send_sem=low_s.at[kind, off], recv_sem=low_r.at[kind, off],
            device_id={"tensor": lax.rem(me + off, nt)}, device_id_type=MESH)

    def send_parts(kind):
        for off in range(1, nt):
            part_copy(kind, off, lax.rem(me + off, nt), me).start()

    def sum_parts(kind):
        total = packed[kind, me]
        for off in range(1, nt):
            sender = lax.rem(me + nt - off, nt)
            part_copy(kind, off, me, sender).wait_recv()
            total = total + landed[kind, sender]
        low[kind, me] = total.astype(BF16)
        for off in range(1, nt):
            low_copy(kind, off, me).start()

    def get_low(kind):
        for off in range(1, nt):
            low_copy(kind, off, lax.rem(me + nt - off, nt)).wait_recv()
        return low[kind].astype(F32).reshape(chunk_rows, LANES)

    def dy_copy(h, way, slot, to):
        block = dy.at[slot, pl.ds(h * half, half)]
        return pltpu.make_async_remote_copy(
            src_ref=block, dst_ref=block, send_sem=dy_s.at[h, way], recv_sem=dy_r.at[h, way],
            device_id={"tensor": to}, device_id_type=MESH)

    def away(off, side):
        return lax.rem(chip + off + chips, chips) * 2 + side

    loads[0].wait()
    loads[1].wait()
    project(0, lambda k: dy[me, k * chunk_rows : (k + 1) * chunk_rows, :], u)
    neighbours = (z > 0).astype(jnp.int32) + (z < nz - 1).astype(jnp.int32)
    pl.semaphore_wait(barrier, nt - 1 + neighbours)
    send_parts(0)
    for h in range(HALVES):
        dy_copy(h, 0, me, partner).start()
    loads[2].wait()
    loads[3].wait()
    project(1, lambda k: x[k * chunk_rows : (k + 1) * chunk_rows, :], d)
    send_parts(1)
    sum_parts(0)
    sum_parts(1)
    for h in range(HALVES):
        if h == 0:
            for off in range(1, chips):
                dy_copy(h, off, me, away(off, core)).start()

    home = jnp.zeros((8, rows), F32)
    for a in range(ar // rank):
        home = home + jnp.where(a_t[...] == float(a), pos[a].astype(F32), 0.0)

    def expand(kind, out_t, out):
        got = get_low(kind)
        for k in range(fold):
            at = slice(k * chunk_rows, (k + 1) * chunk_rows)
            rep = spread(jnp.where(group_of == float(k), got, 0.0))
            rep_t = rep.T
            home_k = jnp.broadcast_to(home[0:1, at], (LANES, chunk_rows))
            for j in range(tiles):
                cols = slice(j * LANES, (j + 1) * LANES)
                out_t[cols, at] = jnp.where(
                    home_k == group_t + float(fold * j), rep_t, 0.0).astype(BF16)
                if out is not None:
                    out[at, cols] = jnp.where(
                        ab[at, :] == group_of + float(fold * j), rep, 0.0).astype(BF16)

    def term(c):
        if c < down_chunks:
            block = jnp.dot(ge_t[...], x[:, c * kv : (c + 1) * kv], preferred_element_type=F32)
        else:
            block = jnp.dot(ue_t[...], dy[me], preferred_element_type=F32)
        own[c] = block.reshape(nz, per, kv)

    steps = nz - 1
    sends = chunks * steps

    def right_copy(c, j):
        return pltpu.make_async_remote_copy(
            src_ref=r_out.at[c, j], dst_ref=r_in.at[c, j],
            send_sem=rs_s.at[c, j], recv_sem=rs_r.at[c, j],
            device_id={"dp": lax.rem(z + 1, nz)}, device_id_type=MESH)

    def left_copy(c, j):
        return pltpu.make_async_remote_copy(
            src_ref=l_out.at[c, j], dst_ref=l_in.at[c, j],
            send_sem=ls_s.at[c, j], recv_sem=ls_r.at[c, j],
            device_id={"dp": lax.rem(z + nz - 1, nz)}, device_id_type=MESH)

    def one_way(t, index, first, farther, owner_of, copy, out, inn):
        c = index // steps
        j = owner_of(lax.rem(index, steps))

        @pl.when((index >= 0) & (index < sends))
        def _():
            @pl.when(first)
            def _():
                @pl.when(index >= WINDOW)
                def _():
                    back = index - WINDOW
                    copy(back // steps, owner_of(lax.rem(back, steps))).wait_send()

                out[c, j] = own[c, j].astype(out.dtype)
                copy(c, j).start()

            @pl.when(jnp.logical_not(first))
            def _():
                @pl.when(farther(j) | (j == z))
                def _():
                    copy(c, j).wait_recv()

                @pl.when(farther(j))
                def _():
                    out[c, j] = (own[c, j] + inn[c, j].astype(F32)).astype(out.dtype)
                    copy(c, j).start()

    def slot(t):
        one_way(t, t - z, z == 0, lambda j: j > z, lambda k: nz - 1 - k,
                right_copy, r_out, r_in)
        one_way(t, t - (nz - 1 - z), z == nz - 1, lambda j: j < z, lambda k: k,
                left_copy, l_out, l_in)

    def store(c):
        if c < down_chunks:
            cols = slice(c * kv, (c + 1) * kv)
            return pltpu.make_async_copy(dg.at[:, cols], dg_h.at[:, cols], out_sem.at[HALVES + c])
        return pltpu.make_async_copy(ug, ug_h, out_sem.at[HALVES + c])

    def final(c):
        from_left = jnp.where(z > 0, r_in[c, z].astype(F32), 0.0)
        from_right = jnp.where(z < nz - 1, l_in[c, z].astype(F32), 0.0)
        total = own[c, z] + from_left + from_right
        if c < down_chunks:
            dg[:, c * kv : (c + 1) * kv] = total
        else:
            ug[...] = total
        store(c).start()

    def frozen(source, h, cols):
        at = pl.ds(pl.multiple_of(source * kv, LANES), kv)
        return lax.dot_general(dy[source, pl.ds(h * half, half), :], w[cols, at], LAST,
                               preferred_element_type=F32)

    pieces = 4
    piece = width // pieces

    def near(p):
        if p == 0:
            loads[4].wait()
            for h in range(HALVES):
                dy_copy(h, 0, partner, partner).wait_recv()
        cols = slice(p * piece, (p + 1) * piece)
        for h in range(HALVES):
            at = slice(h * half, (h + 1) * half)
            acc[at, cols] = (
                jnp.dot(ge[at, :], d[:, cols], preferred_element_type=F32)
                + frozen(me, h, cols) + frozen(partner, h, cols)
            )

    def forward(h):
        for off in range(1, chips):
            got = away(-off, core)
            dy_copy(h, off, got, got).wait_recv()
            dy_copy(h, chips - 1 + off, got, partner).start()
            if h + 1 < HALVES:
                dy_copy(h, off, me, away(off, core)).wait_send()
                dy_copy(h + 1, off, me, away(off, core)).start()

    def ig_store(h):
        at = pl.ds(h * half, half)
        return pltpu.make_async_copy(ig.at[at], ig_h.at[at], out_sem.at[h])

    def far(h):
        for off in range(1, chips):
            dy_copy(h, chips - 1 + off, away(-off, 1 - core), partner).wait_recv()

        @pl.loop(0, pieces)
        def _(p):
            at = pl.ds(h * half, half)
            cols = pl.ds(pl.multiple_of(p * piece, LANES), piece)
            total = acc[at, cols]
            for off in range(1, chips):
                for side in (0, 1):
                    total = total + frozen(away(-off, side), h, cols)
            ig[at, cols] = total.astype(BF16)

        ig_store(h).start()

    before = {0: [lambda: term(0)], 1: [lambda: term(1)], 2: [lambda: term(2)],
              5: [lambda: near(0)], 6: [lambda: near(1)], 7: [lambda: near(2)],
              8: [lambda: near(3)], 9: [lambda: forward(0)], 10: [lambda: far(0)],
              14: [lambda: forward(1)], 15: [lambda: far(1)]}
    before[3] = [lambda c=c: term(c) for c in range(3, down_chunks)]
    before[4] = [lambda: expand(1, ue_t, None), lambda: term(down_chunks)]

    expand(0, ge_t, ge)
    done = 0
    reached = 0
    for mark in range(17):
        upto = sends + 1 if mark == 16 else mark * sends // 15
        upto = min(upto, sends + 1)

        def run(lo, hi):
            if hi - lo == 1:
                slot(lo)
            elif hi > lo:
                lax.fori_loop(lo, hi, lambda t, _: (slot(t), 0)[1], 0)

        while reached < upto:
            stop = min(upto, (reached // steps + 1) * steps + 1 if reached % steps else reached + 1)
            if reached % steps:
                stop = min(upto, (reached // steps + 1) * steps)
            run(reached, stop)
            if (stop - 1) % steps == 0 and stop - 1 > 0:
                final((stop - 1) // steps - 1)
                done += 1
            reached = stop
        for work in before.get(mark, ()):
            work()

    for kind in range(2):
        for off in range(1, nt):
            part_copy(kind, off, me, me).wait_send()
            low_copy(kind, off, me).wait_send()
    for h in range(HALVES):
        dy_copy(h, 0, me, partner).wait_send()
        for off in range(1, chips):
            if h == HALVES - 1:
                dy_copy(h, off, me, away(off, core)).wait_send()
            dy_copy(h, chips - 1 + off, me, partner).wait_send()

    @pl.loop(0, sends)
    def _(i):
        c = i // steps
        k = lax.rem(i, steps)

        @pl.when((nz - 1 - k > z) & ((z > 0) | (i >= sends - WINDOW)))
        def _():
            right_copy(c, nz - 1 - k).wait_send()

        @pl.when((k < z) & ((z < nz - 1) | (i >= sends - WINDOW)))
        def _():
            left_copy(c, k).wait_send()

    for h in range(HALVES):
        ig_store(h).wait()
    for c in range(chunks):
        store(c).wait()


def body(stored_input, output_gradient, frozen_key_value, adapter_down_weight,
         adapter_up_weight, token_tenant, adapter_position):
    nt = lax.axis_size("tensor")
    nz = lax.axis_size("dp")
    rows, width = stored_input.shape
    kv = output_gradient.shape[1]
    adapters, rank = adapter_down_weight.shape[:2]
    ar = adapters * rank
    per = ar // nz
    chunks = width // kv + 1
    q = rows * rank // LANES // nt
    ways = nt - 1
    wire = BF16 if nz <= 4 else F32
    dma = pltpu.SemaphoreType.DMA
    hbm = pl.BlockSpec(memory_space=pl.ANY)
    ig, dg, ug = pl.pallas_call(
        functools.partial(kernel, nt, nz, rank),
        out_shape=(
            jax.ShapeDtypeStruct((rows, width), BF16),
            jax.ShapeDtypeStruct((per, width), F32),
            jax.ShapeDtypeStruct((per, kv), F32),
        ),
        in_specs=[hbm] * 5 + [pl.BlockSpec(memory_space=pltpu.VMEM),
                              pl.BlockSpec(memory_space=pltpu.SMEM)],
        out_specs=(hbm, hbm, hbm),
        scratch_shapes=[
            pltpu.VMEM((rows, width), BF16),
            pltpu.VMEM((nt, rows, kv), BF16),
            pltpu.VMEM(frozen_key_value.shape, BF16),
            pltpu.VMEM((ar, width), BF16),
            pltpu.VMEM((ar, kv), BF16),
            pltpu.VMEM((rows, LANES), F32),
            pltpu.VMEM((8, rows), F32),
            pltpu.VMEM((2, nt, q, LANES), F32),
            pltpu.VMEM((2, nt, q, LANES), F32),
            pltpu.VMEM((2, nt, q, LANES), BF16),
            pltpu.VMEM((rows, ar), BF16),
            pltpu.VMEM((ar, rows), BF16),
            pltpu.VMEM((ar, rows), BF16),
            pltpu.VMEM((chunks, nz, per, kv), F32),
            pltpu.VMEM((rows, width), F32),
            pltpu.VMEM((rows, width), BF16),
            pltpu.VMEM((chunks, nz, per, kv), wire),
            pltpu.VMEM((chunks, nz, per, kv), wire),
            pltpu.VMEM((chunks, nz, per, kv), wire),
            pltpu.VMEM((chunks, nz, per, kv), wire),
            pltpu.VMEM((per, width), F32),
            pltpu.VMEM((per, kv), F32),
            dma((5,)),
            dma((2, nt)), dma((2, nt)), dma((2, nt)), dma((2, nt)),
            dma((HALVES, ways)), dma((HALVES, ways)),
            dma((chunks, nz)), dma((chunks, nz)), dma((chunks, nz)), dma((chunks, nz)),
            dma((HALVES + chunks,)),
        ],
        compiler_params=pltpu.CompilerParams(
            collective_id=0, has_side_effects=True, vmem_limit_bytes=60 * 1024 * 1024
        ),
    )(
        stored_input, output_gradient, frozen_key_value,
        adapter_down_weight.reshape(ar, width), adapter_up_weight.reshape(ar, kv),
        token_tenant.reshape(rows // LANES, LANES), adapter_position,
    )
    return ig, dg.reshape(per // rank, rank, width), ug.reshape(per // rank, rank, kv)


def solution(mesh):
    in_specs = (
        P(("groups", "dp"), "tensor"),
        P(("groups", "dp"), "tensor"),
        P("tensor", None),
        P("groups", None, "tensor"),
        P("groups", None, "tensor"),
        P(("groups", "dp"), None),
        P("groups"),
    )
    out_specs = (
        P(("groups", "dp"), "tensor"),
        P(("groups", "dp"), None, "tensor"),
        P(("groups", "dp"), None, "tensor"),
    )
    return jax.shard_map(body, mesh=mesh, in_specs=in_specs, out_specs=out_specs, check_vma=False)
```

time: 198 us -> 76.2 us (0.38)
  matrix products: 69.6 us -> 0 us
  Pallas kernels: 0 us -> 68.9 us
  local copies, waits for them, and re-layouts: 66.5 us -> 6.43 us
  blocking collectives: 29.3 us -> 0 us
  between operations: 15.6 us -> 0.66 us
  other arithmetic: 8.12 us -> 0 us
  waiting for transfers between devices: 7.6 us -> 0 us
    dot_general x8 -> x0, matrix products: 69.6 us -> none  [the longest x1 17.7 us: body(): jnp.dot(placing, stored_input, preferred_element_type=jnp.float32)]
    pallas_call x0 -> x1, Pallas kernels: none -> 68.9 us  [body(): pl.pallas_call(functools.partial(kernel, nt, nz, rank), out_shape=(jax.Sh...]
    reshape x3 -> x0, local copies, waits for them, and re-layouts: 44 us -> none  [the longest x1 23.2 us: body(): adapter_positions = jnp.einsum('akr,ard->akd', rank_gradient, down_positi...]
    psum x1 -> x0, blocking collectives: 29.3 us -> none  [body(): full_u, full_g = lax.psum((part_u, part_g), 'tensor')]
    gather x3 -> x0, local copies, waits for them, and re-layouts: 18.5 us -> none  [the longest x1 17.3 us: body(): adapter_contribution = jnp.take(adapter_positions, position_index, axis=0)]
    reduce_scatter x1 -> x0, waiting for transfers between devices: 6.9 us -> none  [body(): lax.psum_scatter(jnp.concatenate([down_term, up_term], axis=1), 'dp', sca...]
    unnamed x10 -> x7, local copies, waits for them, and re-layouts: 0.03 us -> 6.43 us
    slice x4 -> x0, local copies, waits for them, and re-layouts: 3.89 us -> none  [the longest x1 2.06 us: body(): owned_rows[:, :width_local].reshape(per_owner, rank_extent, width_local)]
  transfers between devices with their start and end apart: 2 -> 0, of which waited for: 1 -> 0; matrix products, arithmetic and copies ran while one was open for 71% -> 0% of each run, Pallas kernels for 0% -> 0%
where the time goes in v1:
time: 76.2 us; the launch traced here: 76 us
  Pallas kernels  68.9 us (90%)
  local copies, waits for them, and re-layouts  6.43 us (8%)
    pallas_call x1, Pallas kernels, body(): pl.pallas_call(functools.partial(kernel, nt, nz, rank), out_shape=(jax.Sh...  68.9 us
    unnamed x7, local copies, waits for them, and re-layouts  6.43 us

profile of v1, /device:TPU:0, one launch (start us, length us, event | category | flops | bytes accessed | tf_op | source)
XLA Modules:
  0.0 76.0 jit_solution(12201323848592125755)
XLA Ops:
  0.6 68.9 %shard_map.94 = (bf16[1024,2048]{1,0:T(8,128)(2,1)}, f32[96,2048]{1,0:T(8,128)}, f32[96,512]{1,0:T(8,128)}) custom-call(bf16[1024,2048]{1,0:T(8,128)(2,1)} %x_h.1, bf16[1024,512]{1,0:T(8,128)(2,1)} %dy_h.1, bf16[2048,2048]{1,0:T(8,128)(2,1)} %w_h.1, bf16[384,2048]{1,0:T(8,128)(2,1)} %bitcast.5, bf16[384,512]{1,0:T(8,128)(2,1)} %bitcast.7, s32[8,128]{1,0:T(8,128)} %bitcast.9, ...), custom_call_target="tpu_custom_call" | custom-call | tf_op jit(solution)/shard_map/pallas_call | solution.py:366
  69.6 0.0 copy-start
  69.6 0.0 copy-start.1
  69.6 4.9 %copy.13 = bf16[1024,2048]{1,0:T(8,128)(2,1)} copy(bf16[1024,2048]{1,0:T(8,128)(2,1)} %get-tuple-element.12) | data formatting | bytes 8388608
  74.5 0.0 copy-done
  74.5 0.9 %copy.14 = f32[3,32,2048]{2,1,0:T(8,128)} copy(f32[3,32,2048]{2,1,0:T(8,128)S(1)} %bitcast.6) | data formatting | bytes 1572864
  75.3 0.0 copy-done.1
  75.3 0.7 copy.15
Async XLA Ops:
  69.6 4.9 %copy-start = (f32[96,2048]{1,0:T(8,128)S(1)}, f32[96,2048]{1,0:T(8,128)}, u32[]{:S(2)}) copy-start(f32[96,2048]{1,0:T(8,128)} %get-tuple-element.7) | copy-start | bytes 2359300
  69.6 5.8 %copy-start.1 = (f32[96,512]{1,0:T(8,128)S(1)}, f32[96,512]{1,0:T(8,128)}, u32[]{:S(2)}) copy-start(f32[96,512]{1,0:T(8,128)} %get-tuple-element.8) | copy-start | bytes 589828

commit v2 on v1

--- a/solution.py
+++ b/solution.py
@@ -14,12 +14,13 @@
 LAST = (((1,), (1,)), ((), ()))
 HALVES = 2
 WINDOW = 3
-
-
-def kernel(nt, nz, rank, x_h, dy_h, w_h, d_h, u_h, tt, pos, ig_h, dg_h, ug_h,
-           x, dy, w, d, u, ab, a_t, packed, landed, low, ge, ge_t, ue_t, own, acc, ig,
-           r_out, r_in, l_out, l_in, dg, ug,
-           load_sem, part_s, part_r, low_s, low_r, dy_s, dy_r, rs_s, rs_r, ls_s, ls_r, out_sem):
+LAG = 3
+
+
+def kernel(nt, nz, rank, x_h, dy_h, w_h, d_h, u_h, tt, pos, ig, dg, ug,
+           x, dy, w, d, u, ab, a_t, packed, landed, low, ge, ge_t, ue_t, own, acc,
+           r_out, r_in, l_out, l_in,
+           load_sem, part_s, part_r, low_s, low_r, dy_s, dy_r, rs_s, rs_r, ls_s, ls_r):
     me = lax.axis_index("tensor")
     z = lax.axis_index("dp")
     rows, width = x.shape
@@ -43,8 +44,8 @@
             [(u_h, u), (dy_h, dy.at[me]), (d_h, d), (x_h, x), (w_h, w)]
         )
     ]
-    for load in loads:
-        load.start()
+    loads[0].start()
+    loads[1].start()
 
     barrier = pltpu.get_barrier_semaphore()
     for off in range(1, nt):
@@ -58,6 +59,9 @@
     @pl.when(z < nz - 1)
     def _():
         pl.semaphore_signal(barrier, inc=1, device_id={"dp": z + 1}, device_id_type=MESH)
+
+    loads[3].start()
+    loads[2].start()
 
     for i in range(rows // LANES):
         row = jnp.broadcast_to(tt[i : i + 1, :].astype(F32), (LANES, LANES))
@@ -133,24 +137,21 @@
     neighbours = (z > 0).astype(jnp.int32) + (z < nz - 1).astype(jnp.int32)
     pl.semaphore_wait(barrier, nt - 1 + neighbours)
     send_parts(0)
-    for h in range(HALVES):
-        dy_copy(h, 0, me, partner).start()
     loads[2].wait()
     loads[3].wait()
     project(1, lambda k: x[k * chunk_rows : (k + 1) * chunk_rows, :], d)
     send_parts(1)
-    sum_parts(0)
-    sum_parts(1)
-    for h in range(HALVES):
-        if h == 0:
-            for off in range(1, chips):
-                dy_copy(h, off, me, away(off, core)).start()
+    loads[4].start()
 
     home = jnp.zeros((8, rows), F32)
     for a in range(ar // rank):
         home = home + jnp.where(a_t[...] == float(a), pos[a].astype(F32), 0.0)
 
-    def expand(kind, out_t, out):
+    sum_parts(0)
+    for h in range(HALVES):
+        dy_copy(h, 0, me, partner).start()
+
+    def expand(kind, out_t):
         got = get_low(kind)
         for k in range(fold):
             at = slice(k * chunk_rows, (k + 1) * chunk_rows)
@@ -161,9 +162,21 @@
                 cols = slice(j * LANES, (j + 1) * LANES)
                 out_t[cols, at] = jnp.where(
                     home_k == group_t + float(fold * j), rep_t, 0.0).astype(BF16)
-                if out is not None:
-                    out[at, cols] = jnp.where(
-                        ab[at, :] == group_of + float(fold * j), rep, 0.0).astype(BF16)
+
+    def expand_rows():
+        got = low[0].astype(F32).reshape(chunk_rows, LANES)
+        for k in range(fold):
+            at = slice(k * chunk_rows, (k + 1) * chunk_rows)
+            rep = spread(jnp.where(group_of == float(k), got, 0.0))
+            for j in range(tiles):
+                ge[at, j * LANES : (j + 1) * LANES] = jnp.where(
+                    ab[at, :] == group_of + float(fold * j), rep, 0.0).astype(BF16)
+
+    def sum_u():
+        sum_parts(1)
+        for h in range(HALVES):
+            for off in range(1, chips):
+                dy_copy(h, off, me, away(off, core)).start()
 
     def term(c):
         if c < down_chunks:
@@ -205,28 +218,27 @@
 
             @pl.when(jnp.logical_not(first))
             def _():
-                @pl.when(farther(j) | (j == z))
+                @pl.when(farther(j))
                 def _():
                     copy(c, j).wait_recv()
-
-                @pl.when(farther(j))
-                def _():
                     out[c, j] = (own[c, j] + inn[c, j].astype(F32)).astype(out.dtype)
                     copy(c, j).start()
 
     def slot(t):
-        one_way(t, t - z, z == 0, lambda j: j > z, lambda k: nz - 1 - k,
+        one_way(t, t - LAG * z, z == 0, lambda j: j > z, lambda k: nz - 1 - k,
                 right_copy, r_out, r_in)
-        one_way(t, t - (nz - 1 - z), z == nz - 1, lambda j: j < z, lambda k: k,
+        one_way(t, t - LAG * (nz - 1 - z), z == nz - 1, lambda j: j < z, lambda k: k,
                 left_copy, l_out, l_in)
 
-    def store(c):
-        if c < down_chunks:
-            cols = slice(c * kv, (c + 1) * kv)
-            return pltpu.make_async_copy(dg.at[:, cols], dg_h.at[:, cols], out_sem.at[HALVES + c])
-        return pltpu.make_async_copy(ug, ug_h, out_sem.at[HALVES + c])
-
     def final(c):
+        @pl.when(z > 0)
+        def _():
+            right_copy(c, z).wait_recv()
+
+        @pl.when(z < nz - 1)
+        def _():
+            left_copy(c, z).wait_recv()
+
         from_left = jnp.where(z > 0, r_in[c, z].astype(F32), 0.0)
         from_right = jnp.where(z < nz - 1, l_in[c, z].astype(F32), 0.0)
         total = own[c, z] + from_left + from_right
@@ -234,7 +246,6 @@
             dg[:, c * kv : (c + 1) * kv] = total
         else:
             ug[...] = total
-        store(c).start()
 
     def frozen(source, h, cols):
         at = pl.ds(pl.multiple_of(source * kv, LANES), kv)
@@ -262,13 +273,6 @@
             got = away(-off, core)
             dy_copy(h, off, got, got).wait_recv()
             dy_copy(h, chips - 1 + off, got, partner).start()
-            if h + 1 < HALVES:
-                dy_copy(h, off, me, away(off, core)).wait_send()
-                dy_copy(h + 1, off, me, away(off, core)).start()
-
-    def ig_store(h):
-        at = pl.ds(h * half, half)
-        return pltpu.make_async_copy(ig.at[at], ig_h.at[at], out_sem.at[h])
 
     def far(h):
         for off in range(1, chips):
@@ -284,39 +288,30 @@
                     total = total + frozen(away(-off, side), h, cols)
             ig[at, cols] = total.astype(BF16)
 
-        ig_store(h).start()
-
-    before = {0: [lambda: term(0)], 1: [lambda: term(1)], 2: [lambda: term(2)],
-              5: [lambda: near(0)], 6: [lambda: near(1)], 7: [lambda: near(2)],
-              8: [lambda: near(3)], 9: [lambda: forward(0)], 10: [lambda: far(0)],
-              14: [lambda: forward(1)], 15: [lambda: far(1)]}
-    before[3] = [lambda c=c: term(c) for c in range(3, down_chunks)]
-    before[4] = [lambda: expand(1, ue_t, None), lambda: term(down_chunks)]
-
-    expand(0, ge_t, ge)
-    done = 0
+
+    before = {0: [lambda: term(0)], 1: [sum_u, lambda: term(1)],
+              3: [expand_rows],
+              4: [lambda: expand(1, ue_t), lambda: term(down_chunks)],
+              5: [lambda: near(0)], 6: [lambda: near(1)],
+              7: [lambda: near(2)], 8: [lambda: near(3), lambda: forward(0)], 10: [lambda: far(0)],
+              12: [lambda: forward(1)], 15: [lambda: far(1)]}
+    before[2] = [lambda c=c: term(c) for c in range(2, down_chunks)]
+
+    expand(0, ge_t)
     reached = 0
+    slots = max(sends, (chunks - 1) * steps + LAG * (nz - 2) + 1)
     for mark in range(17):
-        upto = sends + 1 if mark == 16 else mark * sends // 15
-        upto = min(upto, sends + 1)
-
-        def run(lo, hi):
-            if hi - lo == 1:
-                slot(lo)
-            elif hi > lo:
-                lax.fori_loop(lo, hi, lambda t, _: (slot(t), 0)[1], 0)
-
-        while reached < upto:
-            stop = min(upto, (reached // steps + 1) * steps + 1 if reached % steps else reached + 1)
-            if reached % steps:
-                stop = min(upto, (reached // steps + 1) * steps)
-            run(reached, stop)
-            if (stop - 1) % steps == 0 and stop - 1 > 0:
-                final((stop - 1) // steps - 1)
-                done += 1
-            reached = stop
+        upto = slots if mark == 16 else mark * sends // 15
+        if upto - reached == 1:
+            slot(reached)
+        elif upto > reached:
+            lax.fori_loop(reached, upto, lambda t, _: (slot(t), 0)[1], 0)
+        reached = upto
         for work in before.get(mark, ()):
             work()
+
+    for c in range(chunks):
+        final(c)
 
     for kind in range(2):
         for off in range(1, nt):
@@ -325,8 +320,7 @@
     for h in range(HALVES):
         dy_copy(h, 0, me, partner).wait_send()
         for off in range(1, chips):
-            if h == HALVES - 1:
-                dy_copy(h, off, me, away(off, core)).wait_send()
+            dy_copy(h, off, me, away(off, core)).wait_send()
             dy_copy(h, chips - 1 + off, me, partner).wait_send()
 
     @pl.loop(0, sends)
@@ -341,11 +335,6 @@
         @pl.when((k < z) & ((z < nz - 1) | (i >= sends - WINDOW)))
         def _():
             left_copy(c, k).wait_send()
-
-    for h in range(HALVES):
-        ig_store(h).wait()
-    for c in range(chunks):
-        store(c).wait()
 
 
 def body(stored_input, output_gradient, frozen_key_value, adapter_down_weight,
@@ -366,13 +355,13 @@
     ig, dg, ug = pl.pallas_call(
         functools.partial(kernel, nt, nz, rank),
         out_shape=(
-            jax.ShapeDtypeStruct((rows, width), BF16),
-            jax.ShapeDtypeStruct((per, width), F32),
-            jax.ShapeDtypeStruct((per, kv), F32),
+            pltpu.VMEM((rows, width), BF16),
+            pltpu.VMEM((per, width), F32),
+            pltpu.VMEM((per, kv), F32),
         ),
         in_specs=[hbm] * 5 + [pl.BlockSpec(memory_space=pltpu.VMEM),
                               pl.BlockSpec(memory_space=pltpu.SMEM)],
-        out_specs=(hbm, hbm, hbm),
+        out_specs=(pl.BlockSpec(memory_space=pltpu.VMEM),) * 3,
         scratch_shapes=[
             pltpu.VMEM((rows, width), BF16),
             pltpu.VMEM((nt, rows, kv), BF16),
@@ -389,21 +378,17 @@
             pltpu.VMEM((ar, rows), BF16),
             pltpu.VMEM((chunks, nz, per, kv), F32),
             pltpu.VMEM((rows, width), F32),
-            pltpu.VMEM((rows, width), BF16),
             pltpu.VMEM((chunks, nz, per, kv), wire),
             pltpu.VMEM((chunks, nz, per, kv), wire),
             pltpu.VMEM((chunks, nz, per, kv), wire),
             pltpu.VMEM((chunks, nz, per, kv), wire),
-            pltpu.VMEM((per, width), F32),
-            pltpu.VMEM((per, kv), F32),
             dma((5,)),
             dma((2, nt)), dma((2, nt)), dma((2, nt)), dma((2, nt)),
             dma((HALVES, ways)), dma((HALVES, ways)),
             dma((chunks, nz)), dma((chunks, nz)), dma((chunks, nz)), dma((chunks, nz)),
-            dma((HALVES + chunks,)),
         ],
         compiler_params=pltpu.CompilerParams(
-            collective_id=0, has_side_effects=True, vmem_limit_bytes=60 * 1024 * 1024
+            collective_id=0, has_side_effects=True, vmem_limit_bytes=52 * 1024 * 1024
         ),
     )(
         stored_input, output_gradient, frozen_key_value,

time: 76.2 us -> 58.3 us (0.77)
  Pallas kernels: 68.9 us -> 53.9 us
  local copies, waits for them, and re-layouts: 6.43 us -> 3.57 us
    pallas_call x1, Pallas kernels: 68.9 us -> 53.9 us  [body(): pl.pallas_call(functools.partial(kernel, nt, nz, rank), out_shape=(pltpu....]
    unnamed x7 -> x3, local copies, waits for them, and re-layouts: 6.43 us -> 3.57 us
where the time goes in v2:
time: 58.3 us; the launch traced here: 58.1 us
  Pallas kernels  53.9 us (92%)
  local copies, waits for them, and re-layouts  3.57 us (6%)
  between operations  0.64 us (1%)
    pallas_call x1, Pallas kernels, body(): pl.pallas_call(functools.partial(kernel, nt, nz, rank), out_shape=(pltpu....  53.9 us
    unnamed x3, local copies, waits for them, and re-layouts  3.57 us

profile of v2, /device:TPU:0, one launch (start us, length us, event | category | flops | bytes accessed | tf_op | source)
XLA Modules:
  0.0 58.1 jit_solution(11302370095959033404)
XLA Ops:
  0.6 53.9 %shard_map.94 = (bf16[1024,2048]{1,0:T(8,128)(2,1)S(1)}, f32[96,2048]{1,0:T(8,128)S(1)}, f32[96,512]{1,0:T(8,128)S(1)}) custom-call(bf16[1024,2048]{1,0:T(8,128)(2,1)} %x_h.1, bf16[1024,512]{1,0:T(8,128)(2,1)} %dy_h.1, bf16[2048,2048]{1,0:T(8,128)(2,1)} %w_h.1, bf16[384,2048]{1,0:T(8,128)(2,1)} %bitcast.7, bf16[384,512]{1,0:T(8,128)(2,1)} %bitcast.8, ...), custom_call_target="tpu_custom_call" | custom-call | tf_op jit(solution)/shard_map/pallas_call | solution.py:355
  54.5 2.0 %copy.13 = bf16[1024,2048]{1,0:T(8,128)(2,1)} copy(bf16[1024,2048]{1,0:T(8,128)(2,1)S(1)} %get-tuple-element.9) | data formatting | bytes 8388608
  56.5 0.9 %copy.14 = f32[3,32,2048]{2,1,0:T(8,128)} copy(f32[3,32,2048]{2,1,0:T(8,128)S(1)} %bitcast.5) | data formatting | bytes 1572864
  57.4 0.7 %copy.15 = f32[3,32,512]{2,1,0:T(8,128)} copy(f32[3,32,512]{2,1,0:T(8,128)S(1)} %bitcast.6) | data formatting | bytes 393216

commit v3 on v2

--- a/solution.py
+++ b/solution.py
@@ -14,7 +14,7 @@
 LAST = (((1,), (1,)), ((), ()))
 HALVES = 2
 WINDOW = 3
-LAG = 3
+LAG = 2
 
 
 def kernel(nt, nz, rank, x_h, dy_h, w_h, d_h, u_h, tt, pos, ig, dg, ug,
@@ -289,7 +289,7 @@
             ig[at, cols] = total.astype(BF16)
 
 
-    before = {0: [lambda: term(0)], 1: [sum_u, lambda: term(1)],
+    before = {0: [lambda: term(0), sum_u], 1: [lambda: term(1)],
               3: [expand_rows],
               4: [lambda: expand(1, ue_t), lambda: term(down_chunks)],
               5: [lambda: near(0)], 6: [lambda: near(1)],

time: 58.3 us -> 57.7 us (0.990)
  Pallas kernels: 53.9 us -> 53.3 us
where the time goes in v3:
time: 57.7 us; the launch traced here: 57.5 us
  Pallas kernels  53.3 us (92%)
  local copies, waits for them, and re-layouts  3.57 us (6%)
  between operations  0.64 us (1%)
    pallas_call x1, Pallas kernels, body(): pl.pallas_call(functools.partial(kernel, nt, nz, rank), out_shape=(pltpu....  53.3 us
    unnamed x3, local copies, waits for them, and re-layouts  3.57 us

profile of v3, /device:TPU:0, one launch (start us, length us, event | category | flops | bytes accessed | tf_op | source)
XLA Modules:
  0.0 57.5 jit_solution(17826178603510541399)
XLA Ops:
  0.6 53.3 %shard_map.94 = (bf16[1024,2048]{1,0:T(8,128)(2,1)S(1)}, f32[96,2048]{1,0:T(8,128)S(1)}, f32[96,512]{1,0:T(8,128)S(1)}) custom-call(bf16[1024,2048]{1,0:T(8,128)(2,1)} %x_h.1, bf16[1024,512]{1,0:T(8,128)(2,1)} %dy_h.1, bf16[2048,2048]{1,0:T(8,128)(2,1)} %w_h.1, bf16[384,2048]{1,0:T(8,128)(2,1)} %bitcast.7, bf16[384,512]{1,0:T(8,128)(2,1)} %bitcast.8, ...), custom_call_target="tpu_custom_call" | custom-call | tf_op jit(solution)/shard_map/pallas_call | solution.py:355
  54.0 2.0 %copy.13 = bf16[1024,2048]{1,0:T(8,128)(2,1)} copy(bf16[1024,2048]{1,0:T(8,128)(2,1)S(1)} %get-tuple-element.9) | data formatting | bytes 8388608
  56.0 0.9 %copy.14 = f32[3,32,2048]{2,1,0:T(8,128)} copy(f32[3,32,2048]{2,1,0:T(8,128)S(1)} %bitcast.5) | data formatting | bytes 1572864
  56.9 0.7 %copy.15 = f32[3,32,512]{2,1,0:T(8,128)} copy(f32[3,32,512]{2,1,0:T(8,128)S(1)} %bitcast.6) | data formatting | bytes 393216
